TPU v7x, 256 devices: a whole 4x4x8 slice. The times are simulated.
256 devices in a mesh: row: 16 (over x, y), col: 8 (over z_lo, core), tp: 2 (over z_hi).
Axes of the slice: x: 4, y: 4, z: 8 (z_hi: 2, z_lo: 4; z = z_hi * 4 + z_lo), core: 2. Of those that a mesh axis runs over, the one named last changes fastest.
Arguments:
- patches: bfloat16 [512, 128, 1536], P(('row', 'col')), may hold values from -6 to 6
- counts: int32 [512], P(('row', 'col')), may hold values from 16 to 128
- text_tokens: bfloat16 [512, 64, 1536], P(('col', 'row')), may hold values from -6 to 6
- partner: int32 [512], replicated, may hold values from 0 to 511, each once
- scale: float32 [1], replicated, may hold values from 4 to 16
- shift: float32 [1], replicated, may hold values from -6 to -2
- img_w_in: bfloat16 [1536, 4096], P('col', 'tp'), may hold values from -0.15625 to 0.15625
- img_w_out: bfloat16 [4096, 1536], P('tp', 'col'), may hold values from -0.09375 to 0.09375
- txt_w_in: bfloat16 [1536, 4096], P('row', 'tp'), may hold values from -0.15625 to 0.15625
- txt_w_out: bfloat16 [4096, 1536], P('tp', 'row'), may hold values from -0.09375 to 0.09375
Outputs:
- grad_patches: bfloat16 [512, 128, 1536], P(('row', 'col'), None, 'tp')
- grad_text: bfloat16 [512, 64, 1536], P(('col', 'row'), None, 'tp')
All inputs are finite; a program needn't handle non-finite values.
Results may differ from a plain program's by a relative error of at most 0.0065.
Values may be sent and summed in bfloat16 or wider, within the bound.
A program may use at most 128 MiB of HBM per device.

v0:
```python
import jax
import jax.numpy as jnp
from jax import lax
from jax.sharding import PartitionSpec as P


def silu_grad(value):
    sig = jax.nn.sigmoid(value)
    return sig * (1.0 + value * (1.0 - sig))


def layer_forward(tokens, counts, w_in, w_out):
    nb, slots, width = tokens.shape
    mask = (jnp.arange(slots)[None, :] < counts[:, None]).astype(jnp.float32)
    cnt = counts.astype(jnp.float32)[:, None]
    pre = jnp.dot(
        tokens.reshape(nb * slots, width), w_in, preferred_element_type=jnp.float32
    ).reshape(nb, slots, -1)
    pooled_hidden = (jnp.sum(mask[:, :, None] * jax.nn.silu(pre), 1) / cnt).astype(jnp.bfloat16)
    pooled_x = jnp.sum(mask[:, :, None] * tokens.astype(jnp.float32), 1) / cnt
    partial_value = jnp.dot(pooled_hidden, w_out, preferred_element_type=jnp.float32)
    return (pre, mask, cnt, pooled_x, partial_value)


def layer_backward(tokens, pre, mask, dtoken, w_in, w_out):
    nb, slots, width = tokens.shape
    dhidden = lax.dot_general(
        dtoken.astype(jnp.bfloat16),
        w_out,
        (((1,), (1,)), ((), ())),
        preferred_element_type=jnp.float32,
    )
    dpre = (mask[:, :, None] * dhidden[:, None, :] * silu_grad(pre)).astype(jnp.bfloat16)
    back = lax.dot_general(
        dpre.reshape(nb * slots, -1),
        w_in,
        (((1,), (1,)), ((), ())),
        preferred_element_type=jnp.float32,
    )
    return back.reshape(nb, slots, width)


def normalize(pooled):
    norm = jnp.sqrt(jnp.sum(pooled * pooled, -1, keepdims=True) + 1e-06)
    return (pooled / norm, norm)


def tile_terms(rows_emb, cols_emb, row_partner, col_ids, temp, bias):
    logits = temp * jnp.dot(rows_emb, cols_emb.T, precision=lax.Precision.HIGHEST) + bias
    sign = jnp.where(row_partner[:, None] == col_ids[None, :], 1.0, -1.0)
    dlogits = -sign * jax.nn.sigmoid(-sign * logits)
    d_rows = temp * jnp.dot(dlogits, cols_emb, precision=lax.Precision.HIGHEST)
    d_cols = temp * jnp.dot(dlogits.T, rows_emb, precision=lax.Precision.HIGHEST)
    return (d_rows, d_cols)


def shards(
    patches, counts, text_tokens, partner, scale, shift, img_w_in, img_w_out, txt_w_in, txt_w_out
):
    per_dev = patches.shape[0]
    width = patches.shape[2]
    nrow = lax.axis_size("row")
    ncol = lax.axis_size("col")
    rindex = lax.axis_index("row")
    cindex = lax.axis_index("col")
    temp = scale[0]
    bias = shift[0]
    w_in_img = lax.all_gather(img_w_in, "col", axis=0, tiled=True)
    w_out_img = lax.all_gather(img_w_out, "col", axis=1, tiled=True)
    w_in_txt = lax.all_gather(txt_w_in, "row", axis=0, tiled=True)
    w_out_txt = lax.all_gather(txt_w_out, "row", axis=1, tiled=True)
    text_counts = jnp.full((per_dev,), text_tokens.shape[1], jnp.int32)
    pre_img, mask_img, cnt_img, px_img, part_img = layer_forward(
        patches, counts, w_in_img, w_out_img
    )
    pre_txt, mask_txt, cnt_txt, px_txt, part_txt = layer_forward(
        text_tokens, text_counts, w_in_txt, w_out_txt
    )
    sum_img, sum_txt = lax.psum((part_img, part_txt), "tp")
    emb_img, norm_img = normalize(px_img + sum_img)
    emb_txt, norm_txt = normalize(px_txt + sum_txt)
    image_shard = rindex * ncol + cindex
    cols_emb = lax.all_gather(emb_txt, ("row", "col"), axis=0, tiled=True)
    row_partner = lax.dynamic_slice_in_dim(partner, image_shard * per_dev, per_dev, 0)
    places = jnp.arange(nrow * ncol * per_dev, dtype=jnp.int32)
    block = places // per_dev
    col_ids = (block % ncol * nrow + block // ncol) * per_dev + places % per_dev
    d_img, d_cols = tile_terms(emb_img, cols_emb, row_partner, col_ids, temp, bias)
    d_txt = lax.psum_scatter(d_cols, ("row", "col"), scatter_dimension=0, tiled=True)
    dp_img = (d_img - emb_img * jnp.sum(emb_img * d_img, -1, keepdims=True)) / norm_img
    dp_txt = (d_txt - emb_txt * jnp.sum(emb_txt * d_txt, -1, keepdims=True)) / norm_txt
    dtok_img = dp_img / cnt_img
    dtok_txt = dp_txt / cnt_txt
    back_img = layer_backward(patches, pre_img, mask_img, dtok_img, w_in_img, w_out_img)
    back_txt = layer_backward(text_tokens, pre_txt, mask_txt, dtok_txt, w_in_txt, w_out_txt)
    sum_back_img, sum_back_txt = (
        lax.psum_scatter(back_img, "tp", scatter_dimension=2, tiled=True),
        lax.psum_scatter(back_txt, "tp", scatter_dimension=2, tiled=True),
    )
    half = width // lax.axis_size("tp")
    offset = lax.axis_index("tp") * half
    own_img = lax.dynamic_slice_in_dim(dtok_img, offset, half, 1)
    own_txt = lax.dynamic_slice_in_dim(dtok_txt, offset, half, 1)
    grad_patches = (mask_img[:, :, None] * own_img[:, None, :] + sum_back_img).astype(jnp.bfloat16)
    grad_text = (mask_txt[:, :, None] * own_txt[:, None, :] + sum_back_txt).astype(jnp.bfloat16)
    return (grad_patches, grad_text)


def solution(mesh):
    return jax.shard_map(
        shards,
        mesh=mesh,
        in_specs=(
            P(("row", "col"), None, None),
            P(("row", "col")),
            P(("col", "row"), None, None),
            P(),
            P(),
            P(),
            P("col", "tp"),
            P("tp", "col"),
            P("row", "tp"),
            P("tp", "row"),
        ),
        out_specs=(P(("row", "col"), None, "tp"), P(("col", "row"), None, "tp")),
        check_vma=False,
    )
```

profile of v0, /device:TPU:1, one launch (start us, length us, event | category | flops | bytes accessed | tf_op | source)
XLA Modules:
  0.0 1981.1 jit_solution(16525979640284789132)
XLA Ops:
  7.2 0.7 all-gather.7.cloned.1.call-update
  7.9 0.0 all-gather.9.cloned.1.call-start
  8.0 0.7 all-gather.9.cloned.1.call-update
  8.7 0.0 all-gather.11.cloned.1.call-start
  8.7 0.7 all-gather.11.cloned.1.call-update
  9.4 0.0 all-gather.13.cloned.1.call-start
  9.4 0.5 all-gather.13.cloned.1.call-update
  10.0 0.0 all-gather.15.cloned.1.call-start
  10.0 0.7 convert_element_type.53
  10.7 1.4 multiply_reduce_fusion.3
  12.1 0.1 fusion.44
  12.2 73.5 %all-gather.7.cloned.1.call-done = bf16[1536,2048]{1,0:T(8,128)(2,1)} async-done(((bf16[192,2048]{1,0:T(8,128)(2,1)}), bf16[1536,2048]{1,0:T(8,128)(2,1)}) %all-gather.7.cloned.1.call-update) | async-done | bytes 6291472 | tf_op jit(solution)/shard_map/all_gather | solution.py:68
  85.6 8.1 multiply_reduce_fusion
  93.8 66.6 %all-gather.9.cloned.1.call-done = bf16[2048,1536]{0,1:T(8,128)(2,1)} async-done(((bf16[2048,192]{0,1:T(8,128)(2,1)}), bf16[2048,1536]{0,1:T(8,128)(2,1)}) %all-gather.9.cloned.1.call-update) | async-done | bytes 6291472 | tf_op jit(solution)/shard_map/all_gather | solution.py:69
  160.4 4.6 fusion.21
  165.0 65.3 %all-gather.11.cloned.1.call-done = bf16[1536,2048]{1,0:T(8,128)(2,1)} async-done(((bf16[96,2048]{1,0:T(8,128)(2,1)}), bf16[1536,2048]{1,0:T(8,128)(2,1)}) %all-gather.11.cloned.1.call-update) | async-done | bytes 6291472 | tf_op jit(solution)/shard_map/all_gather | solution.py:70
  230.3 6.1 multiply_reduce_fusion.2
  236.4 62.3 %all-gather.13.cloned.1.call-done = bf16[2048,1536]{0,1:T(8,128)(2,1)} async-done(((bf16[2048,96]{0,1:T(8,128)(2,1)}), bf16[2048,1536]{0,1:T(8,128)(2,1)}) %all-gather.13.cloned.1.call-update) | async-done | bytes 6291472 | tf_op jit(solution)/shard_map/all_gather | solution.py:71
  298.8 4.5 fusion.22
  303.3 15.2 all-reduce.1
  318.5 0.1 multiply_reduce_fusion.6
  318.7 0.7 broadcast_divide_fusion
  319.4 0.2 all-reduce.4.cloned.1.call-start
  320.9 0.8 dynamic_slice.9
  321.7 0.4 multiply_reduce_fusion.1
  322.1 0.2 multiply_reduce_fusion.7
  322.3 193.3 %all-gather.15.cloned.1.call-done = f32[128,4,1536]{2,1,0:T(4,128)} async-done(((f32[1,4,1536]{2,1,0:T(4,128)}), f32[128,4,1536]{2,1,0:T(4,128)}) %all-gather.15.cloned.1.call-update) | async-done | bytes 3145744 | tf_op jit(solution)/shard_map/all_gather | solution.py:83
  515.6 3.2 reshape.117
  518.8 2.7 fusion.17
  521.5 4.3 convolution_multiply_fusion
  525.9 0.0 reduce-scatter.3.cloned.1.call-start
  525.9 1.7 multiply_reduce_fusion.5
  527.6 0.1 subtract_divide_fusion
  527.7 3.9 fusion.27
  531.6 0.1 copy-done.6
  531.7 8.4 fusion.4
  540.2 0.3 reduce-scatter.5.cloned.1.call-start
  540.5 0.4 copy-done.4
  540.8 0.6 dynamic-slice
  542.1 1289.1 %all-reduce.4.cloned.1.call-done = f32[512,1536]{1,0:T(8,128)} async-done(((f32[512,1536]{1,0:T(8,128)}), f32[512,1536]{1,0:T(8,128)}) %all-reduce.4.cloned.1.call-update) | async-done | bytes 3145744
  1831.2 0.9 multiply_reduce_fusion.4
  1832.1 0.9 divide_multiply_fusion
  1833.0 3.9 fusion.25
  1836.9 6.1 fusion
  1843.0 78.0 %reduce-scatter.3.cloned.1.call-done = f32[4,128,768]{2,1,0:T(8,128)} async-done(((f32[4,128,1536]{2,1,0:T(8,128)}), f32[4,128,768]{2,1,0:T(8,128)}) %reduce-scatter.3.cloned.1.call-update) | async-done | bytes 1572880 | tf_op jit(solution)/shard_map/reduce_scatter | solution.py:97
  1921.1 2.5 add_convert_fusion
  1923.6 48.6 %reduce-scatter.5.cloned.1.call-done = f32[4,64,768]{2,1,0:T(8,128)} async-done(((f32[4,64,1536]{2,1,0:T(8,128)}), f32[4,64,768]{2,1,0:T(8,128)}) %reduce-scatter.5.cloned.1.call-update) | async-done | bytes 786448 | tf_op jit(solution)/shard_map/reduce_scatter | solution.py:98
  1972.2 2.0 add_convert_fusion.1
  (23 shorter events, 0.2 us)
Async XLA Ops:
  7.2 4.9 copy-start.3
  7.2 78.5 %copy-start = (bf16[4,128,1536]{2,1,0:T(8,128)(2,1)S(1)}, bf16[4,128,1536]{2,1,0:T(8,128)(2,1)}, u32[]{:S(2)}) copy-start(bf16[4,128,1536]{2,1,0:T(8,128)(2,1)} %param.10) | copy-start | bytes 4718596
  7.2 78.4 %all-gather.7.cloned.1.call-start = ((), (), s32[]{:S(2)}) async-start(), calls=%async_computation.2 | async-start | bytes 7077888 | tf_op jit(solution)/shard_map/all_gather | solution.py:68
  7.9 152.5 %all-gather.9.cloned.1.call-start = ((), (), s32[]{:S(2)}) async-start(), calls=%async_computation.3 | async-start | bytes 7077888 | tf_op jit(solution)/shard_map/all_gather | solution.py:69
  8.7 221.6 %all-gather.11.cloned.1.call-start = ((), (), s32[]{:S(2)}) async-start(), calls=%async_computation.4 | async-start | bytes 6684672 | tf_op jit(solution)/shard_map/all_gather | solution.py:70
  9.4 289.4 %all-gather.13.cloned.1.call-start = ((), (), s32[]{:S(2)}) async-start(), calls=%async_computation.5 | async-start | bytes 6684672 | tf_op jit(solution)/shard_map/all_gather | solution.py:71
  10.0 505.7 %all-gather.15.cloned.1.call-start = ((), (), s32[]{:S(2)}) async-start(), calls=%async_computation.8 | async-start | bytes 3170304 | tf_op jit(solution)/shard_map/all_gather | solution.py:83
  160.4 69.9 %copy-start.1 = (bf16[4,64,1536]{2,1,0:T(8,128)(2,1)S(1)}, bf16[4,64,1536]{2,1,0:T(8,128)(2,1)}, u32[]{:S(2)}) copy-start(bf16[4,64,1536]{2,1,0:T(8,128)(2,1)} %param.12) | copy-start | bytes 2359300
  319.4 1511.8 %all-reduce.4.cloned.1.call-start = ((), (), s32[]{:S(2)}) async-start(), calls=%async_computation.9 | async-start | bytes 6291456
  525.9 1395.2 %reduce-scatter.3.cloned.1.call-start = ((), (), s32[]{:S(2)}) async-start(), calls=%async_computation.6 | async-start | bytes 4718592 | tf_op jit(solution)/shard_map/reduce_scatter | solution.py:97
  527.7 4.0 copy-start.6
  540.2 0.7 copy-start.4
  540.2 1291.1 %copy-start.2 = (f32[4,1536]{1,0:T(4,128)S(1)}, f32[4,1536]{1,0:T(4,128)}, u32[]{:S(2)}) copy-start(f32[4,1536]{1,0:T(4,128)} %broadcast_divide_fusion) | copy-start | bytes 73732
  540.2 1432.0 %reduce-scatter.5.cloned.1.call-start = ((), (), s32[]{:S(2)}) async-start(), calls=%async_computation.7 | async-start | bytes 2359296 | tf_op jit(solution)/shard_map/reduce_scatter | solution.py:98
  1833.0 3.9 copy-start.5
Sparse Core Ops, SparseCore 0:
  9.8 75.7 all-gather.6
  87.4 72.9 all-gather.8
  162.9 67.3 all-gather.10
  232.6 66.0 all-gather.12
  319.5 196.1 all-gather.14
  526.0 1305.1 all-reduce.3
  1833.9 87.1 reduce-scatter.2
  1923.6 48.5 reduce-scatter.4
where the time goes:
time: 1980 us
  waiting for transfers between devices  1880 us (95%)
  matrix products  54.3 us (3%)
    unnamed x9, waiting for transfers between devices  1290 us
    all_gather x1, waiting for transfers between devices, shards(): cols_emb = lax.all_gather(emb_txt, ('row', 'col'), axis=0, tiled=True)  193 us
    reduce_scatter x1, waiting for transfers between devices, shards(): lax.psum_scatter(back_img, 'tp', scatter_dimension=2, tiled=True)  78 us
    all_gather x1, waiting for transfers between devices, shards(): w_in_img = lax.all_gather(img_w_in, 'col', axis=0, tiled=True)  73.5 us
    all_gather x1, waiting for transfers between devices, shards(): w_out_img = lax.all_gather(img_w_out, 'col', axis=1, tiled=True)  66.6 us
    all_gather x1, waiting for transfers between devices, shards(): w_in_txt = lax.all_gather(txt_w_in, 'row', axis=0, tiled=True)  65.3 us
    all_gather x1, waiting for transfers between devices, shards(): w_out_txt = lax.all_gather(txt_w_out, 'row', axis=1, tiled=True)  62.3 us
    reduce_scatter x1, waiting for transfers between devices, shards(): lax.psum_scatter(back_txt, 'tp', scatter_dimension=2, tiled=True)  48.6 us
  transfers between devices with their start and end apart: 8, of which 8 were waited for; matrix products, arithmetic and copies ran while one was open for 3% of the time, Pallas kernels for 0%

commit v1 on v0

v1 whole, which is shorter than its diff:
```python
import jax
import jax.numpy as jnp
from jax import lax
from jax.experimental import pallas as pl
from jax.experimental.pallas import tpu as pltpu
from jax.sharding import PartitionSpec as P

F32, BF16 = jnp.float32, jnp.bfloat16
TXT, IMG = 0, 1
NROW, NCOL, SIDE = 16, 8, 4
D, HID, HALF, PAD = 1536, 2048, 768, 2048
IPD, SLOTS, TOKENS = 4, 128, 64
MI, MT = IPD * SLOTS, IPD * TOKENS
PX, AA, CC, EE, FF = range(5)
NT = (((1,), (1,)), ((), ()))


def mm(a, b):
    return jnp.dot(a, b, preferred_element_type=F32)


def mm_nt(a, b):
    return lax.dot_general(a, b, NT, preferred_element_type=F32)


def split(v):
    hi = v.astype(BF16)
    return hi, (v - hi.astype(F32)).astype(BF16)


def kernel(
    counts, partner, scale, shift, xi_h, xt_h, wii_h, woi_h, wit_h, wot_h,
    oi_h, ot_h,
    wi, wt, xi, xt, woi_raw, wot_raw, woi, wot, sel,
    sp_i, sp_t, hp_i, hp_t, acc_i, acc_t, dpre_i, dpre_t, out_i, out_t,
    px_i, px_t, pxall_i, pxall_t, a_i, a_t, stage, ph,
    bs_i, bs_t, br_i, br_t, c_i, c_t, pool_i, pool_t,
    es_i, es_t, e_i, e_t, fs_i, fs_t, f_i, f_t, tail, f2s, f2r, dh_i, dh_t, dtp,
    gs, gr, zs, zr, ls, ms, mr, bs, br,
):
    r, c, t = lax.axis_index("row"), lax.axis_index("col"), lax.axis_index("tp")
    x, y = lax.div(r, SIDE), lax.rem(r, SIDE)
    zlo, k = lax.div(c, 2), lax.rem(c, 2)
    u = 1 - t
    pf = x * (1 - k) + y * k
    qf = y * (1 - k) + x * k
    am, bm = 4 - 3 * k, 1 + 3 * k

    def row_of(f, q):
        return f * am + q * bm

    def turn(v, by):
        return lax.rem(v + by, SIDE)

    def remote(src, dst, ssem, rsem, dev):
        return pltpu.make_async_remote_copy(
            src_ref=src, dst_ref=dst, send_sem=ssem, recv_sem=rsem,
            device_id=dev, device_id_type=pl.DeviceIdType.MESH,
        )

    own_cols = pl.ds(pl.multiple_of(128 * r, 128), 128)
    own_rows = pl.ds(pl.multiple_of(48 * k, 16), 48)

    locals_ = [
        pltpu.make_async_copy(wit_h.at[own_rows], wt.at[t, r, k], ls.at[0]),
        pltpu.make_async_copy(wii_h.at[:, own_cols], wi.at[t, r, zlo, k], ls.at[1]),
        pltpu.make_async_copy(xi_h, xi, ls.at[2]),
        pltpu.make_async_copy(xt_h, xt, ls.at[3]),
        pltpu.make_async_copy(woi_h, woi_raw, ls.at[4]),
        pltpu.make_async_copy(wot_h, wot_raw, ls.at[5]),
    ]
    for copy in locals_:
        copy.start()

    barrier = pltpu.get_barrier_semaphore()

    def greet(dev):
        pl.semaphore_signal(barrier, inc=1, device_id=dev, device_id_type=pl.DeviceIdType.MESH)

    @pl.loop(1, NCOL)
    def _(i):
        greet({"col": lax.rem(c + i, NCOL)})

    @pl.loop(1, NROW)
    def _(i):
        greet({"row": lax.rem(r + i, NROW)})

    @pl.loop(0, SIDE)
    def _(i):
        greet({"col": 2 * turn(zlo, i) + k, "tp": u})

    pl.semaphore_wait(barrier, 7 + 15 + 4)

    def z_img_same(i, slot):
        return remote(
            wii_h.at[:, own_cols], wi.at[t, r, slot, k], zs.at[i], zr.at[i], {"col": 2 * turn(zlo, i) + k}
        )

    def z_img_other(i, half, slot):
        return remote(
            wii_h.at[:, own_cols], wi.at[half, r, slot, k], zs.at[4 + i], zr.at[4 + i],
            {"col": 2 * turn(zlo, i) + k, "tp": u},
        )

    def z_txt(half):
        return remote(wit_h.at[own_rows], wt.at[half, r, k], zs.at[8], zr.at[8], {"tp": u})

    @pl.loop(1, SIDE)
    def _(i):
        z_img_same(i, zlo).start()

    def z_later():
        z_txt(t).start()

        @pl.loop(0, SIDE)
        def _(i):
            z_img_other(i, t, zlo).start()

    dev_p = [{"row": row_of(turn(pf, 1), qf)}, {"row": row_of(turn(pf, 3), qf)}]
    dev_q = [{"row": row_of(pf, turn(qf, 1))}, {"row": row_of(pf, turn(qf, 3))}]
    sibling = {"col": c + 1 - 2 * k}

    class Batch:
        def __init__(self, n, tower, half):
            self.n, self.tower, self.half = n, tower, half

        def shard(self, row, core=None):
            core = k if core is None else core
            if self.tower == TXT:
                return wt.at[self.half, row, core]
            return wi.at[self.half, row, :, core]

        def part(self, row, h):
            if self.tower == TXT:
                return wt.at[self.half, row, k, :, pl.ds(1024 * h, 1024)]
            return wi.at[self.half, row, pl.ds(2 * h, 2), k]

        def copy(self, index, ref, dev):
            return remote(ref, ref, gs.at[self.n, index], gr.at[self.n, index], dev)

        def to_sibling(self, row):
            self.copy(16 + row, self.shard(row), sibling).start()

        def spread(self, j):
            row = row_of(turn(pf, j), qf)
            ref = self.shard(row)
            self.copy(4 + 2 * j, ref, dev_q[0]).start()
            self.copy(5 + 2 * j, ref, dev_q[1]).start()
            self.to_sibling(row)

        def s1(self):
            ref = self.shard(r)
            self.copy(0, ref, dev_p[0]).start()
            self.copy(1, ref, dev_p[1]).start()
            self.spread(0)

        def s2(self):
            left, right = row_of(turn(pf, 3), qf), row_of(turn(pf, 1), qf)
            self.copy(0, self.shard(left), dev_p[0]).wait_recv()
            self.copy(2, self.part(left, 0), dev_p[0]).start()
            self.copy(1, self.shard(right), dev_p[1]).wait_recv()
            self.copy(3, self.part(right, 1), dev_p[1]).start()
            self.spread(3)
            self.spread(1)

        def s2b(self):
            far = row_of(turn(pf, 2), qf)
            self.copy(2, self.part(far, 0), dev_p[0]).wait_recv()
            self.copy(3, self.part(far, 1), dev_p[1]).wait_recv()
            self.spread(2)

        def s3(self):
            for j in (0, 3, 1, 2):
                for way, at in ((0, 3), (1, 1)):
                    row = row_of(turn(pf, j), turn(qf, at))
                    ref = self.shard(row)
                    self.copy(4 + 2 * j + way, ref, dev_q[way]).wait_recv()
                    if (j in (0, 1)) == (way == 0):
                        self.copy(12 + j, ref, dev_q[way]).start()
                    self.to_sibling(row)

        def s4(self):
            for j in (0, 3, 1, 2):
                row = row_of(turn(pf, j), turn(qf, 2))
                self.copy(12 + j, self.shard(row), dev_q[0]).wait_recv()
                self.to_sibling(row)

        def from_sibling(self):
            @pl.loop(0, NROW)
            def _(row):
                self.copy(16 + row, self.shard(row, 1 - k), sibling).wait_recv()

        def drain(self):
            for j in (0, 1):
                self.copy(j, self.shard(r), dev_p[j]).wait_send()
                self.copy(2 + j, self.part(r, j), dev_p[j]).wait_send()

            @pl.loop(4, 32)
            def _(i):
                self.copy(i, self.shard(r), dev_q[0]).wait_send()

    t0, i0, t1, i1 = Batch(0, TXT, t), Batch(1, IMG, t), Batch(2, TXT, u), Batch(3, IMG, u)

    def send_img(stage_id, src, dst):
        @pl.loop(1, NCOL)
        def _(i):
            to = lax.rem(c + i, NCOL)
            remote(src(to), dst.at[c], ms.at[stage_id, i], mr.at[stage_id, i], {"col": to}).start()

    def send_txt(stage_id, src, dst):
        @pl.loop(1, NROW)
        def _(i):
            to = lax.rem(r + i, NROW)
            remote(src(to), dst.at[r], ms.at[stage_id, 8 + i], mr.at[stage_id, 8 + i], {"row": to}).start()

    def recv_img(stage_id, dst):
        @pl.loop(1, NCOL)
        def _(i):
            ref = dst.at[lax.rem(c + NCOL - i, NCOL)]
            remote(ref, ref, ms.at[stage_id, i], mr.at[stage_id, i], {"col": lax.rem(c + i, NCOL)}).wait_recv()

    def recv_txt(stage_id, dst):
        @pl.loop(1, NROW)
        def _(i):
            ref = dst.at[lax.rem(r + NROW - i, NROW)]
            remote(ref, ref, ms.at[stage_id, 8 + i], mr.at[stage_id, 8 + i], {"row": lax.rem(r + i, NROW)}).wait_recv()

    def drain_small(stage_id, src_i, src_t):
        @pl.loop(1, NCOL)
        def _(i):
            remote(src_i.at[c], src_i.at[c], ms.at[stage_id, i], mr.at[stage_id, i], {"col": lax.rem(c + i, NCOL)}).wait_send()

        @pl.loop(1, NROW)
        def _(i):
            remote(
                src_t.at[r], src_t.at[r], ms.at[stage_id, 8 + i], mr.at[stage_id, 8 + i], {"row": lax.rem(r + i, NROW)}
            ).wait_send()

    def live(i, width):
        return lax.broadcasted_iota(jnp.int32, (SLOTS, width), 0) < counts[i]

    def counted(i, width):
        return jnp.full((1, width), counts[i], jnp.int32).astype(F32)

    def local_part():
        d = lax.broadcasted_iota(jnp.int32, (384, 512), 0)
        e = lax.broadcasted_iota(jnp.int32, (384, 512), 1)
        hit = ((e & 127) < 96) & (d == (e >> 7) * 96 + (e & 127))
        sel[...] = jnp.where(hit, 1.0, 0.0).astype(BF16)
        for copy in locals_[2:]:
            copy.wait()
        row = lax.broadcasted_iota(jnp.int32, (8, MI), 0)
        tok = lax.broadcasted_iota(jnp.int32, (8, MI), 1)
        limit = jnp.zeros((8, MI), jnp.int32)
        for i in range(IPD):
            limit = jnp.where(row == i, counts[i], limit)
        mask_i = jnp.where((tok >= SLOTS * row) & (tok < SLOTS * row + limit), 1.0, 0.0).astype(BF16)
        row = lax.broadcasted_iota(jnp.int32, (8, MT), 0)
        tok = lax.broadcasted_iota(jnp.int32, (8, MT), 1)
        mask_t = jnp.where((tok >= TOKENS * row) & (tok < TOKENS * row + TOKENS), 1.0, 0.0).astype(BF16)
        sub = lax.broadcasted_iota(jnp.int32, (8, 128), 0)
        cnt = jnp.full((8, 128), 1, jnp.int32)
        for i in range(IPD):
            cnt = jnp.where(sub == i, counts[i], cnt)
        cnt = cnt.astype(F32)
        px_i[c, :, PAD:] = cnt[0:IPD]
        sums_i = mm(mask_i, xi[...]) / cnt[:, 0:1]
        sums_t = mm(mask_t, xt[...]) / float(TOKENS)
        for sums, dst, at in ((sums_i, px_i, c), (sums_t, px_t, r)):
            hi, lo = split(sums)
            both = jnp.concatenate([hi.astype(F32), lo.astype(F32)], axis=0).astype(BF16)
            for g in range(4):
                wide = mm(both[:, 384 * g:384 * (g + 1)], sel[...])
                dst[at, :, 512 * g:512 * (g + 1)] = (wide[0:8] + wide[8:16])[0:IPD]
        send_img(PX, lambda to: px_i.at[c], px_i)
        send_txt(PX, lambda to: px_t.at[r], px_t)

    def pad_out():
        woi[...] = mm(woi_raw[...], jnp.concatenate([sel[0:192, 0:128], sel[0:192, 128:256]], axis=1)).astype(BF16)
        wot[...] = mm(wot_raw[...], sel[0:96, 0:128]).astype(BF16)
        acc_i[...] = jnp.zeros_like(acc_i)
        acc_t[...] = jnp.zeros_like(acc_t)

    def fwd_img(half, pooled):
        @pl.loop(0, 8)
        def _(p):
            w = jnp.concatenate([wi[half, 2 * p + j].reshape(D, 128) for j in (0, 1)], axis=1)
            pre = mm(xi[...], w)
            for i in range(IPD):
                v = 0.5 * pre[SLOTS * i:SLOTS * (i + 1)]
                th = jnp.tanh(v)
                on = live(i, 256)
                slope = 0.5 * (1.0 + th) * (1.0 + v * (1.0 - th))
                sp_i[half, p, SLOTS * i:SLOTS * (i + 1), :] = jnp.where(on, slope, 0.0)
                if pooled:
                    total = jnp.sum(jnp.where(on, v + v * th, 0.0), axis=0, keepdims=True)
                    hp_i[p, i:i + 1, :] = total / counted(i, 256)

    def fwd_txt(half, pooled):
        @pl.loop(0, 4)
        def _(n):
            w = wt[half, :, :, :, pl.ds(pl.multiple_of(512 * n, 512), 512)].reshape(D, 512)
            pre = mm(xt[...], w)
            for i in range(IPD):
                v = 0.5 * pre[TOKENS * i:TOKENS * (i + 1)]
                th = jnp.tanh(v)
                sp_t[half, n, TOKENS * i:TOKENS * (i + 1), :] = 0.5 * (1.0 + th) * (1.0 + v * (1.0 - th))
                if pooled:
                    hp_t[n, i:i + 1, :] = jnp.sum(v + v * th, axis=0, keepdims=True) / float(TOKENS)

    def send_hidden_img():
        for q in range(4):
            for h in range(2):
                stage[4 * q:4 * q + 4, 256 * h:256 * (h + 1)] = hp_i[2 * q + h, 0:IPD]
        a_i[c] = stage[...].astype(BF16)
        send_img(AA, lambda to: a_i.at[c], a_i)

    def send_hidden_txt():
        for q in range(4):
            stage[4 * q:4 * q + 4, :] = hp_t[q, 0:IPD]
        a_t[r] = stage[...].astype(BF16)
        send_txt(AA, lambda to: a_t.at[r], a_t)

    def projected(src, peers, w):
        for p in range(peers):
            block = src[p].astype(F32)
            for q in range(4):
                ph[4 * p:4 * p + 4, 512 * q:512 * (q + 1)] = block[4 * q:4 * q + 4]
        return mm(ph[0:4 * peers].astype(BF16), w[...])

    def to_partner(index, src, dst):
        return remote(src, dst, bs.at[index], br.at[index], {"tp": u})

    def norm_of(pool):
        inv = lax.rsqrt(jnp.sum(pool * pool, axis=-1, keepdims=True) + 1e-6)
        return pool * inv, inv

    def loss():
        for p in range(NCOL):
            pxall_i[4 * p:4 * p + 4, :] = px_i[p]
        for p in range(NROW):
            pxall_t[4 * p:4 * p + 4, :] = px_t[p]
        for p in range(NCOL):
            at = slice(256 * p, 256 * (p + 1))
            pool_i[:, at] = pxall_i[:, at] + c_i[p].astype(F32)
        for p in range(NROW):
            at = slice(128 * p, 128 * (p + 1))
            pool_t[:, at] = pxall_t[:, at] + c_t[p].astype(F32)
        emb_i, inv_i = norm_of(pool_i[...])
        emb_t, inv_t = norm_of(pool_t[...])
        ih, il = split(emb_i)
        th, tl = split(emb_t)
        ni, nt = 32, 64
        one = mm_nt(jnp.concatenate([ih, il], axis=0), th)
        cos = one[0:ni] + one[ni:] + mm_nt(ih, tl)
        two = mm_nt(jnp.concatenate([th, tl], axis=0), ih)
        cos_t = two[0:nt] + two[nt:] + mm_nt(th, il)
        temp, bias = scale[0], shift[0]
        row = lax.broadcasted_iota(jnp.int32, (ni, nt), 0)
        lane = lax.broadcasted_iota(jnp.int32, (nt, ni), 1)
        mate = jnp.zeros((ni, nt), jnp.int32)
        mate_t = jnp.zeros((nt, ni), jnp.int32)
        for i in range(ni):
            text = partner[r * ni + i]
            mate = jnp.where(row == i, text, mate)
            mate_t = jnp.where(lane == i, text, mate_t)

        def slopes(value, other, ids):
            sign = jnp.where(other == ids, 1.0, -1.0)
            return -sign * jax.nn.sigmoid(-sign * (temp * value + bias))

        dl = slopes(cos, mate, c * nt + lax.broadcasted_iota(jnp.int32, (ni, nt), 1))
        dl_t = slopes(cos_t, mate_t, c * nt + lax.broadcasted_iota(jnp.int32, (nt, ni), 0))
        dh, dlo = split(dl)
        one = mm(jnp.concatenate([dh, dlo], axis=0), th)
        g_i = one[0:ni] + one[ni:] + mm(dh, tl)
        dh, dlo = split(dl_t)
        two = mm(jnp.concatenate([dh, dlo], axis=0), ih)
        g_t = two[0:nt] + two[nt:] + mm(dh, il)
        q_i = jnp.sum(dl * cos, axis=-1, keepdims=True)
        q_t = jnp.sum(dl_t * cos_t, axis=-1, keepdims=True)
        part_i = (g_i - emb_i * q_i) * (temp * inv_i / pxall_i[:, PAD:PAD + 1])
        part_t = (g_t - emb_t * q_t) * (temp * inv_t * (1.0 / TOKENS))
        for p in range(NCOL):
            es_i[p] = part_i[:, 256 * p:256 * (p + 1)].astype(BF16)
        for p in range(NROW):
            es_t[p] = part_t[:, 128 * p:128 * (p + 1)].astype(BF16)
        e_i[c] = es_i[c]
        e_t[r] = es_t[r]
        send_img(EE, lambda to: es_i.at[to], e_i)
        send_txt(EE, lambda to: es_t.at[to], e_t)

    def dhidden(src, peers, w, dst, wide):
        total = src[0].astype(F32)
        for p in range(1, peers):
            total = total + src[p].astype(F32)
        hi, lo = split(total)
        hidden = mm_nt(hi, w[...])
        hi, lo = hi.astype(F32), lo.astype(F32)
        for p in range(peers):
            rows = slice(4 * p, 4 * p + 4)
            for q in range(4):
                stage[4 * q:4 * q + 4, :] = hidden[rows, 512 * q:512 * (q + 1)]
            dst[p, :, 0:512] = stage[...].astype(BF16)
            tail[0:4, :] = hi[rows, 0:128]
            tail[8:12, :] = lo[rows, 0:128]
            if wide:
                tail[4:8, :] = hi[rows, 128:256]
                tail[12:16, :] = lo[rows, 128:256]
            dst[p, :, 512:640] = tail[...].astype(BF16)

    def hidden_sum(src, peers, dst):
        total = src[0, :, 0:512].astype(F32)
        for p in range(1, peers):
            total = total + src[p, :, 0:512].astype(F32)
        stage[...] = total
        for q in range(4):
            dst[4 * t + q, 0:IPD, :] = stage[4 * q:4 * q + 4, :]
        return total.astype(BF16)

    def hidden_other(src, dst):
        stage[...] = src.astype(F32)
        for q in range(4):
            dst[4 * u + q, 0:IPD, :] = stage[4 * q:4 * q + 4, :]

    def back_img(half):
        @pl.loop(0, 4)
        def _(n):
            for h in range(2):
                for i in range(IPD):
                    at = slice(SLOTS * i, SLOTS * (i + 1))
                    slope = sp_i[half, 2 * n + h, at, :]
                    dpre_i[at, 256 * h:256 * (h + 1)] = (
                        slope * dh_i[4 * half + n, i:i + 1, 256 * h:256 * (h + 1)]
                    ).astype(BF16)
            w = jnp.concatenate([wi[half, 4 * n + j, pl.ds(2 * t, 2)].reshape(HALF, 128) for j in range(4)], axis=1)
            acc_i[...] += mm_nt(dpre_i[...], w)

    def back_txt(half):
        @pl.loop(0, 4)
        def _(n):
            for i in range(IPD):
                at = slice(TOKENS * i, TOKENS * (i + 1))
                dpre_t[at, :] = (sp_t[half, n, at, :] * dh_t[4 * half + n, i:i + 1, :]).astype(BF16)
            w = wt[half, pl.ds(8 * t, 8), :, :, pl.ds(pl.multiple_of(512 * n, 512), 512)].reshape(HALF, 512)
            acc_t[...] += mm_nt(dpre_t[...], w)

    def token_part(src, wide):
        if wide:
            for p in range(4):
                block = src[4 * t + p, :, 512:640].astype(F32)
                for h in range(2):
                    at = slice(256 * p + 128 * h, 256 * p + 128 * (h + 1))
                    dtp[0:4, at] = block[4 * h:4 * h + 4]
                    dtp[8:12, at] = block[8 + 4 * h:12 + 4 * h]
        else:
            for p in range(8):
                dtp[:, 128 * p:128 * (p + 1)] = src[8 * t + p, :, 512:640].astype(F32)
        natural = [mm_nt(dtp[:, 512 * g:512 * (g + 1)].astype(BF16), sel[...]) for g in range(2)]
        natural = jnp.concatenate(natural, axis=1)
        return natural[0:8] + natural[8:16]

    def finish_txt():
        token = token_part(f_t, False)
        for i in range(IPD):
            at = slice(TOKENS * i, TOKENS * (i + 1))
            out_t[at, :] = (acc_t[at, :] + token[i:i + 1]).astype(BF16)
        copy = pltpu.make_async_copy(out_t, ot_h, ls.at[6])
        copy.start()
        return copy

    def finish_img():
        token = token_part(f_i, True)
        for i in range(IPD):
            at = slice(SLOTS * i, SLOTS * (i + 1))
            out_i[at, :] = (acc_i[at, :] + jnp.where(live(i, HALF), token[i:i + 1], 0.0)).astype(BF16)
        copy = pltpu.make_async_copy(out_i, oi_h, ls.at[7])
        copy.start()
        return copy

    def await_z_same():
        @pl.loop(1, SIDE)
        def _(i):
            z_img_same(i, turn(zlo, SIDE - i)).wait_recv()

    def await_z_other():
        @pl.loop(0, SIDE)
        def _(i):
            z_img_other(i, u, turn(zlo, SIDE - i)).wait_recv()

    locals_[0].wait()
    t0.s1()
    z_later()
    tail[...] = jnp.zeros_like(tail)
    dtp[...] = jnp.zeros_like(dtp)
    local_part()
    t0.s2()
    t0.s2b()
    locals_[1].wait()
    await_z_same()
    i0.s1()
    pad_out()
    t0.s3()
    i0.s2()
    t0.s4()
    i0.s2b()
    t0.from_sibling()
    fwd_txt(t, True)
    send_hidden_txt()
    i0.s3()
    z_txt(u).wait_recv()
    t1.s1()
    i0.s4()
    t1.s2()
    t1.s2b()
    await_z_other()
    i1.s1()
    i0.from_sibling()
    fwd_img(t, True)
    send_hidden_img()
    recv_txt(AA, a_t)
    bs_t[...] = projected(a_t, NROW, wot)
    to_partner(1, bs_t, br_t).start()
    recv_img(AA, a_i)
    bs_i[...] = projected(a_i, NCOL, woi)
    to_partner(0, bs_i, br_i).start()
    i1.s2()
    to_partner(1, bs_t, br_t).wait_recv()
    c_t[r] = (bs_t[...] + br_t[...]).astype(BF16)
    send_txt(CC, lambda to: c_t.at[r], c_t)
    to_partner(0, bs_i, br_i).wait_recv()
    c_i[c] = (bs_i[...] + br_i[...]).astype(BF16)
    send_img(CC, lambda to: c_i.at[c], c_i)
    t1.s3()
    i1.s2b()
    recv_img(PX, px_i)
    recv_txt(PX, px_t)
    recv_img(CC, c_i)
    recv_txt(CC, c_t)
    loss()
    t1.s4()
    recv_img(EE, e_i)
    dhidden(e_i, NCOL, woi, fs_i, True)
    f_i[c] = fs_i[c]
    send_img(FF, lambda to: fs_i.at[to], f_i)
    recv_txt(EE, e_t)
    dhidden(e_t, NROW, wot, fs_t, False)
    f_t[r] = fs_t[r]
    send_txt(FF, lambda to: fs_t.at[to], f_t)
    i1.s3()
    recv_img(FF, f_i)
    f2s[0:16, :] = hidden_sum(f_i, NCOL, dh_i)
    recv_txt(FF, f_t)
    f2s[16:32, :] = hidden_sum(f_t, NROW, dh_t)
    to_partner(2, f2s, f2r).start()
    back_txt(t)
    i1.s4()
    back_img(t)
    t1.from_sibling()
    fwd_txt(u, False)
    to_partner(2, f2s, f2r).wait_recv()
    hidden_other(f2r[0:16, :], dh_i)
    hidden_other(f2r[16:32, :], dh_t)
    back_txt(u)
    done_t = finish_txt()
    i1.from_sibling()
    fwd_img(u, False)
    back_img(u)
    done_i = finish_img()

    @pl.loop(1, SIDE)
    def _(i):
        z_img_same(i, zlo).wait_send()

    @pl.loop(0, SIDE)
    def _(i):
        z_img_other(i, t, zlo).wait_send()

    z_txt(t).wait_send()
    for batch in (t0, i0, t1, i1):
        batch.drain()
    to_partner(0, bs_i, br_i).wait_send()
    to_partner(1, bs_t, br_t).wait_send()
    to_partner(2, f2s, f2r).wait_send()
    drain_small(PX, px_i, px_t)
    drain_small(AA, a_i, a_t)
    drain_small(CC, c_i, c_t)
    drain_small(EE, es_i, es_t)
    drain_small(FF, fs_i, fs_t)
    done_t.wait()
    done_i.wait()


def vm(*shape, dtype=F32):
    return pltpu.VMEM(shape, dtype)


SCRATCH = [
    vm(2, NROW, 4, 2, 192, 128, dtype=BF16), vm(2, NROW, 2, 48, HID, dtype=BF16),
    vm(MI, D, dtype=BF16), vm(MT, D, dtype=BF16),
    vm(HID, 192, dtype=BF16), vm(HID, 96, dtype=BF16), vm(HID, 256, dtype=BF16), vm(HID, 128, dtype=BF16),
    vm(384, 512, dtype=BF16),
    vm(2, 8, MI, 256), vm(2, 4, MT, 512), vm(8, 8, 256), vm(4, 8, 512),
    vm(MI, HALF), vm(MT, HALF), vm(MI, 512, dtype=BF16), vm(MT, 512, dtype=BF16),
    vm(MI, HALF, dtype=BF16), vm(MT, HALF, dtype=BF16),
    vm(NCOL, IPD, PAD + 128), vm(NROW, IPD, PAD), vm(32, PAD + 128), vm(64, PAD),
    vm(NCOL, 16, 512, dtype=BF16), vm(NROW, 16, 512, dtype=BF16), vm(16, 512), vm(64, HID),
    vm(32, 256), vm(64, 128), vm(32, 256), vm(64, 128),
    vm(NCOL, 32, 256, dtype=BF16), vm(NROW, 64, 128, dtype=BF16), vm(32, PAD), vm(64, PAD),
    vm(NCOL, 32, 256, dtype=BF16), vm(NROW, 64, 128, dtype=BF16),
    vm(NCOL, 32, 256, dtype=BF16), vm(NROW, 64, 128, dtype=BF16),
    vm(NCOL, 16, 640, dtype=BF16), vm(NROW, 16, 640, dtype=BF16),
    vm(NCOL, 16, 640, dtype=BF16), vm(NROW, 16, 640, dtype=BF16),
    vm(16, 128), vm(32, 512, dtype=BF16), vm(32, 512, dtype=BF16), vm(8, 8, 512), vm(8, 8, 512), vm(16, 1024),
    pltpu.SemaphoreType.DMA((4, 32)), pltpu.SemaphoreType.DMA((4, 32)),
    pltpu.SemaphoreType.DMA((9,)), pltpu.SemaphoreType.DMA((9,)),
    pltpu.SemaphoreType.DMA((8,)),
    pltpu.SemaphoreType.DMA((5, 24)), pltpu.SemaphoreType.DMA((5, 24)),
    pltpu.SemaphoreType.DMA((3,)), pltpu.SemaphoreType.DMA((3,)),
]


def shards(patches, counts, text, partner, scale, shift, img_w_in, img_w_out, txt_w_in, txt_w_out):
    smem = pl.BlockSpec(memory_space=pltpu.SMEM)
    hbm = pl.BlockSpec(memory_space=pl.ANY)
    grad_i, grad_t = pl.pallas_call(
        kernel,
        out_shape=(jax.ShapeDtypeStruct((MI, HALF), BF16), jax.ShapeDtypeStruct((MT, HALF), BF16)),
        in_specs=[smem] * 4 + [hbm] * 6,
        out_specs=(hbm, hbm),
        scratch_shapes=SCRATCH,
        compiler_params=pltpu.CompilerParams(
            collective_id=0, has_side_effects=True, vmem_limit_bytes=60 * 2**20
        ),
        name="towers",
    )(
        counts, partner, scale, shift, patches.reshape(MI, D), text.reshape(MT, D),
        img_w_in, img_w_out, txt_w_in, txt_w_out,
    )
    return grad_i.reshape(IPD, SLOTS, HALF), grad_t.reshape(IPD, TOKENS, HALF)


def solution(mesh):
    return jax.shard_map(
        shards,
        mesh=mesh,
        in_specs=(
            P(("row", "col"), None, None), P(("row", "col")), P(("col", "row"), None, None), P(), P(), P(),
            P("col", "tp"), P("tp", "col"), P("row", "tp"), P("tp", "row"),
        ),
        out_specs=(P(("row", "col"), None, "tp"), P(("col", "row"), None, "tp")),
        check_vma=False,
    )
```

time: 1980 us -> 134 us (0.07)
  waiting for transfers between devices: 1880 us -> 0 us
  Pallas kernels: 0 us -> 125 us
  matrix products: 54.3 us -> 0 us
    unnamed x9 -> x0, waiting for transfers between devices: 1290 us -> none
    all_gather x5 -> x0, waiting for transfers between devices: 461 us -> none  [the longest x1 193 us: shards(): cols_emb = lax.all_gather(emb_txt, ('row', 'col'), axis=0, tiled=True)]
    reduce_scatter x2 -> x0, waiting for transfers between devices: 127 us -> none  [the longest x1 78 us: shards(): lax.psum_scatter(back_img, 'tp', scatter_dimension=2, tiled=True)]
    pallas_call x0 -> x1, Pallas kernels: none -> 125 us  [shards(): pl.pallas_call(kernel, out_shape=(jax.ShapeDtypeStruct((MI, HALF), BF16),...]
    dot_general x11 -> x0, matrix products: 54.3 us -> none  [the longest x2 14.5 us: layer_backward(): lax.dot_general(dpre.reshape(nb * slots, -1), w_in, (((1,), (1,)), ((), (...]
  transfers between devices with their start and end apart: 8 -> 0, of which waited for: 8 -> 0; matrix products, arithmetic and copies ran while one was open for 3% -> 0% of each run, Pallas kernels for 0% -> 0%
where the time goes in v1:
time: 134 us
  Pallas kernels  125 us (93%)
  local copies, waits for them, and re-layouts  7.07 us (5%)
  between operations  1.94 us (1%)
    pallas_call x1, Pallas kernels, shards(): pl.pallas_call(kernel, out_shape=(jax.ShapeDtypeStruct((MI, HALF), BF16),...  125 us
    unnamed x6, local copies, waits for them, and re-layouts  7.07 us

profile of v1, /device:TPU:1, one launch (start us, length us, event | category | flops | bytes accessed | tf_op | source)
XLA Modules:
  0.0 133.8 jit_solution(17334043997905104742)
XLA Ops:
  1.9 2.0 %copy.13.wot_h = bf16[2048,96]{1,0:T(8,128)(2,1)} copy(bf16[2048,96]{0,1:T(8,128)(2,1)} %param.19) | data formatting | bytes 786432 | tf_op args[9]
  3.9 2.2 %copy.12.woi_h = bf16[2048,192]{1,0:T(8,128)(2,1)} copy(bf16[2048,192]{0,1:T(8,128)(2,1)} %param.17) | data formatting | bytes 1572864 | tf_op args[7]
  6.1 124.7 %towers.1 = (bf16[512,768]{1,0:T(8,128)(2,1)}, bf16[256,768]{1,0:T(8,128)(2,1)}) custom-call(s32[4]{0:T(128)} %counts.1, s32[512]{0:T(512)} %partner.1, f32[1]{0:T(128)S(6)} %copy.16.scale, f32[1]{0:T(128)S(6)} %copy.17.shift, bf16[512,1536]{1,0:T(8,128)(2,1)} %bitcast.4, bf16[256,1536]{1,0:T(8,128)(2,1)} %bitcast.6, bf16[192,2048]{1,0:T(8,128)(2,1)} %wii_h.1, ...), custom_call_target="tpu_custom_call" | custom-call | tf_op jit(solution)/shard_map/towers/pallas_call | solution.py:626
  130.9 0.0 copy-start
  130.9 2.1 %copy.18 = bf16[4,128,768]{2,1,0:T(8,128)(2,1)} copy(bf16[4,128,768]{2,1,0:T(8,128)(2,1)} %bitcast.5) | data formatting | bytes 1572864
  133.0 0.0 copy-done
  133.0 0.7 copy.19
Async XLA Ops:
  130.9 2.1 %copy-start = (bf16[256,768]{1,0:T(8,128)(2,1)S(1)}, bf16[256,768]{1,0:T(8,128)(2,1)}, u32[]{:S(2)}) copy-start(bf16[256,768]{1,0:T(8,128)(2,1)} %get-tuple-element.5) | copy-start | bytes 1179652

commit v2 on v1

--- a/solution.py
+++ b/solution.py
@@ -12,6 +12,7 @@
 IPD, SLOTS, TOKENS = 4, 128, 64
 MI, MT = IPD * SLOTS, IPD * TOKENS
 PX, AA, CC, EE, FF = range(5)
+RHO = 32
 NT = (((1,), (1,)), ((), ()))
 
 
@@ -30,13 +31,13 @@
 
 def kernel(
     counts, partner, scale, shift, xi_h, xt_h, wii_h, woi_h, wit_h, wot_h,
-    oi_h, ot_h,
-    wi, wt, xi, xt, woi_raw, wot_raw, woi, wot, sel,
-    sp_i, sp_t, hp_i, hp_t, acc_i, acc_t, dpre_i, dpre_t, out_i, out_t,
-    px_i, px_t, pxall_i, pxall_t, a_i, a_t, stage, ph,
-    bs_i, bs_t, br_i, br_t, c_i, c_t, pool_i, pool_t,
+    out_i, out_t,
+    wi, wz, wt, xi, xt, woi_raw, wot_raw, woi, wot, sel,
+    sp_i, sp_t, hp_i, hp_t, acc_i, acc_t, dpre_i, dpre_t, dpre_i2, dpre_t2,
+    px_i, px_t, pxs_i, pxs_t, pxall_i, pxall_t, a_i, a_t, stage, ph,
+    bs_t, br_t, c_i, c_t, pool_i, pool_t,
     es_i, es_t, e_i, e_t, fs_i, fs_t, f_i, f_t, tail, f2s, f2r, dh_i, dh_t, dtp,
-    gs, gr, zs, zr, ls, ms, mr, bs, br,
+    gs, gr, zs, zr, ls, os_, ms, mr, bs, br, xs, xr,
 ):
     r, c, t = lax.axis_index("row"), lax.axis_index("col"), lax.axis_index("tp")
     x, y = lax.div(r, SIDE), lax.rem(r, SIDE)
@@ -61,17 +62,29 @@
     own_cols = pl.ds(pl.multiple_of(128 * r, 128), 128)
     own_rows = pl.ds(pl.multiple_of(48 * k, 16), 48)
 
+    whole_rows, block_rows = pl.ds(192 - RHO, RHO), pl.ds(0, 192 - RHO)
+
+    def own_block(i):
+        cols = pl.ds(pl.multiple_of(128 * i, 128), 128)
+        return pltpu.make_async_copy(wii_h.at[block_rows, cols], wi.at[t, i, 0, k, block_rows], os_.at[i])
+
     locals_ = [
         pltpu.make_async_copy(wit_h.at[own_rows], wt.at[t, r, k], ls.at[0]),
-        pltpu.make_async_copy(wii_h.at[:, own_cols], wi.at[t, r, zlo, k], ls.at[1]),
-        pltpu.make_async_copy(xi_h, xi, ls.at[2]),
+        pltpu.make_async_copy(wii_h.at[whole_rows], wz.at[0, k], ls.at[1]),
         pltpu.make_async_copy(xt_h, xt, ls.at[3]),
         pltpu.make_async_copy(woi_h, woi_raw, ls.at[4]),
         pltpu.make_async_copy(wot_h, wot_raw, ls.at[5]),
     ]
+    for i in range(SIDE):
+        span = pl.ds(pl.multiple_of(384 * turn(zlo, i), 128), 384)
+        locals_.append(pltpu.make_async_copy(xi_h.at[:, span], xi.at[:, 384 * i:384 * (i + 1)], ls.at[8 + i]))
     for copy in locals_:
         copy.start()
 
+    @pl.loop(0, NROW)
+    def _(i):
+        own_block(i).start()
+
     barrier = pltpu.get_barrier_semaphore()
 
     def greet(dev):
@@ -85,15 +98,21 @@
     def _(i):
         greet({"row": lax.rem(r + i, NROW)})
 
-    @pl.loop(0, SIDE)
-    def _(i):
-        greet({"col": 2 * turn(zlo, i) + k, "tp": u})
-
-    pl.semaphore_wait(barrier, 7 + 15 + 4)
+    @pl.loop(0, NCOL)
+    def _(i):
+        greet({"col": lax.rem(c + i, NCOL), "tp": u})
+
+    pl.semaphore_wait(barrier, 7 + 15 + 8)
 
     def z_img_same(i, slot):
         return remote(
-            wii_h.at[:, own_cols], wi.at[t, r, slot, k], zs.at[i], zr.at[i], {"col": 2 * turn(zlo, i) + k}
+            wii_h.at[block_rows, own_cols], wi.at[t, r, slot, k, block_rows], zs.at[i], zr.at[i],
+            {"col": 2 * turn(zlo, i) + k},
+        )
+
+    def z_img_whole(i, slot):
+        return remote(
+            wii_h.at[whole_rows], wz.at[slot, k], zs.at[8 + i], zr.at[8 + i], {"col": 2 * turn(zlo, i) + k}
         )
 
     def z_img_other(i, half, slot):
@@ -102,38 +121,60 @@
             {"col": 2 * turn(zlo, i) + k, "tp": u},
         )
 
-    def z_txt(half):
-        return remote(wit_h.at[own_rows], wt.at[half, r, k], zs.at[8], zr.at[8], {"tp": u})
+    def z_txt(half, to, sem):
+        return remote(wit_h.at[own_rows], wt.at[half, r, k], zs.at[sem], zr.at[8], {"col": 2 * to + k, "tp": u})
+
+    def z_txt_each(act):
+        @pl.when(zlo == 3)
+        def _():
+            act(z_txt(t, 0, 8))
+            act(z_txt(t, 1, 0))
+
+        @pl.when(zlo == 0)
+        def _():
+            act(z_txt(t, 3, 8))
+            act(z_txt(t, 2, 0))
+
+    sibling = {"col": c + 1 - 2 * k}
+
+    def whole_to_sibling(i, core):
+        ref = wz.at[i, core]
+        return remote(ref, ref, zs.at[12 + i], zr.at[12 + i], sibling)
+
+    def own_to_sibling(core):
+        ref = wi.at[t, :, 0, core, block_rows]
+        return remote(ref, ref, zs.at[16], zr.at[16], sibling)
 
     @pl.loop(1, SIDE)
     def _(i):
-        z_img_same(i, zlo).start()
+        z_img_same(i, SIDE - i).start()
 
     def z_later():
-        z_txt(t).start()
-
         @pl.loop(0, SIDE)
         def _(i):
-            z_img_other(i, t, zlo).start()
+            z_img_other(i, t, lax.rem(SIDE - i, SIDE)).start()
 
     dev_p = [{"row": row_of(turn(pf, 1), qf)}, {"row": row_of(turn(pf, 3), qf)}]
     dev_q = [{"row": row_of(pf, turn(qf, 1))}, {"row": row_of(pf, turn(qf, 3))}]
-    sibling = {"col": c + 1 - 2 * k}
-
     class Batch:
         def __init__(self, n, tower, half):
             self.n, self.tower, self.half = n, tower, half
+            own = n == 1
+            self.first, self.rows = (1, 192 - RHO) if own else (0, 192)
 
         def shard(self, row, core=None):
             core = k if core is None else core
             if self.tower == TXT:
                 return wt.at[self.half, row, core]
-            return wi.at[self.half, row, :, core]
+            return self.block(row, core, 0, self.rows)
+
+        def block(self, row, core, start, rows):
+            return wi.at[self.half, row, self.first:SIDE, core, pl.ds(start, rows)]
 
         def part(self, row, h):
             if self.tower == TXT:
                 return wt.at[self.half, row, k, :, pl.ds(1024 * h, 1024)]
-            return wi.at[self.half, row, pl.ds(2 * h, 2), k]
+            return self.block(row, k, self.rows // 2 * h, self.rows // 2)
 
         def copy(self, index, ref, dev):
             return remote(ref, ref, gs.at[self.n, index], gr.at[self.n, index], dev)
@@ -169,8 +210,8 @@
             self.copy(3, self.part(far, 1), dev_p[1]).wait_recv()
             self.spread(2)
 
-        def s3(self):
-            for j in (0, 3, 1, 2):
+        def s3(self, *js):
+            for j in js:
                 for way, at in ((0, 3), (1, 1)):
                     row = row_of(turn(pf, j), turn(qf, at))
                     ref = self.shard(row)
@@ -188,7 +229,10 @@
         def from_sibling(self):
             @pl.loop(0, NROW)
             def _(row):
-                self.copy(16 + row, self.shard(row, 1 - k), sibling).wait_recv()
+                self.row_from_sibling(row)
+
+        def row_from_sibling(self, row):
+            self.copy(16 + row, self.shard(row, 1 - k), sibling).wait_recv()
 
         def drain(self):
             for j in (0, 1):
@@ -263,41 +307,76 @@
         for i in range(IPD):
             cnt = jnp.where(sub == i, counts[i], cnt)
         cnt = cnt.astype(F32)
-        px_i[c, :, PAD:] = cnt[0:IPD]
+        for p in range(NCOL):
+            pxs_i[p, :, 256:] = cnt[0:IPD]
         sums_i = mm(mask_i, xi[...]) / cnt[:, 0:1]
         sums_t = mm(mask_t, xt[...]) / float(TOKENS)
-        for sums, dst, at in ((sums_i, px_i, c), (sums_t, px_t, r)):
+        for sums, dst, per in ((sums_i, pxs_i, 256), (sums_t, pxs_t, 128)):
             hi, lo = split(sums)
             both = jnp.concatenate([hi.astype(F32), lo.astype(F32)], axis=0).astype(BF16)
             for g in range(4):
                 wide = mm(both[:, 384 * g:384 * (g + 1)], sel[...])
-                dst[at, :, 512 * g:512 * (g + 1)] = (wide[0:8] + wide[8:16])[0:IPD]
-        send_img(PX, lambda to: px_i.at[c], px_i)
-        send_txt(PX, lambda to: px_t.at[r], px_t)
+                wide = (wide[0:8] + wide[8:16])[0:IPD]
+                first = 2 * turn(zlo, g) if per == 256 else 4 * g
+                for p in range(512 // per):
+                    dst[first + p, :, 0:per] = wide[:, per * p:per * (p + 1)]
+        px_i[c] = pxs_i[c]
+        px_t[r] = pxs_t[r]
+        send_img(PX, lambda to: pxs_i.at[to], px_i)
+        send_txt(PX, lambda to: pxs_t.at[to], px_t)
+
+    def pooled_tokens(src, peers, width, dst):
+        for p in range(peers):
+            dst[4 * p:4 * p + 4, :] = src[p]
+        return dst[:, 0:width]
 
     def pad_out():
-        woi[...] = mm(woi_raw[...], jnp.concatenate([sel[0:192, 0:128], sel[0:192, 128:256]], axis=1)).astype(BF16)
-        wot[...] = mm(wot_raw[...], sel[0:96, 0:128]).astype(BF16)
-        acc_i[...] = jnp.zeros_like(acc_i)
-        acc_t[...] = jnp.zeros_like(acc_t)
-
-    def fwd_img(half, pooled):
-        @pl.loop(0, 8)
-        def _(p):
-            w = jnp.concatenate([wi[half, 2 * p + j].reshape(D, 128) for j in (0, 1)], axis=1)
-            pre = mm(xi[...], w)
-            for i in range(IPD):
-                v = 0.5 * pre[SLOTS * i:SLOTS * (i + 1)]
-                th = jnp.tanh(v)
-                on = live(i, 256)
-                slope = 0.5 * (1.0 + th) * (1.0 + v * (1.0 - th))
-                sp_i[half, p, SLOTS * i:SLOTS * (i + 1), :] = jnp.where(on, slope, 0.0)
-                if pooled:
-                    total = jnp.sum(jnp.where(on, v + v * th, 0.0), axis=0, keepdims=True)
-                    hp_i[p, i:i + 1, :] = total / counted(i, 256)
+        for raw, dst, narrow, wide in ((woi_raw, woi, 192, 256), (wot_raw, wot, 96, 128)):
+            e = lax.broadcasted_iota(jnp.int32, (wide, narrow), 0)
+            d = lax.broadcasted_iota(jnp.int32, (wide, narrow), 1)
+            hit = ((e & 127) < 96) & (d == (e >> 7) * 96 + (e & 127))
+            dst[...] = mm(jnp.where(hit, 1.0, 0.0).astype(BF16), raw[...]).astype(BF16)
+
+    def img_rows(own, half, row, ds):
+        if not own:
+            return jnp.concatenate([wi[half, row, d].reshape(384, 128) for d in ds], axis=0)
+        cols = pl.ds(pl.multiple_of(128 * row, 128), 128)
+        return jnp.concatenate(
+            [v for d in ds for h in (0, 1) for v in (wi[half, row, d, h, block_rows], wz[d, h, :, cols])], axis=0
+        )
+
+    def img_block(own, half, p, pooled):
+        w = jnp.concatenate([img_rows(own, half, 2 * p + j, range(SIDE)) for j in (0, 1)], axis=1)
+        pre = mm(xi[...], w)
+        for i in range(IPD):
+            v = 0.5 * pre[SLOTS * i:SLOTS * (i + 1)]
+            th = jnp.tanh(v)
+            on = live(i, 256)
+            slope = 0.5 * (1.0 + th) * (1.0 + v * (1.0 - th))
+            sp_i[half, p, SLOTS * i:SLOTS * (i + 1), :] = jnp.where(on, slope, 0.0)
+            if pooled:
+                total = jnp.sum(jnp.where(on, v + v * th, 0.0), axis=0, keepdims=True)
+                hp_i[p, i:i + 1, :] = total / counted(i, 256)
+
+    def fwd_img(batch, pooled, first, last):
+        near = lax.div(y, 2)
+
+        def block_of(n):
+            m, e = lax.rem(n, 4), lax.div(n, 4)
+            along = m + lax.div(m, 2) * (1 - 2 * lax.rem(m, 2))
+            return 2 * turn(x, along) + near + e * (1 - 2 * near)
+
+        @pl.loop(first, last)
+        def _(n):
+            ps = [block_of(2 * n), block_of(2 * n + 1)]
+            for p in ps:
+                batch.row_from_sibling(2 * p)
+                batch.row_from_sibling(2 * p + 1)
+            for p in ps:
+                img_block(batch.n == 1, batch.half, p, pooled)
 
     def fwd_txt(half, pooled):
-        @pl.loop(0, 4)
+        @pl.loop(0, 4, unroll=2)
         def _(n):
             w = wt[half, :, :, :, pl.ds(pl.multiple_of(512 * n, 512), 512)].reshape(D, 512)
             pre = mm(xt[...], w)
@@ -326,10 +405,28 @@
             block = src[p].astype(F32)
             for q in range(4):
                 ph[4 * p:4 * p + 4, 512 * q:512 * (q + 1)] = block[4 * q:4 * q + 4]
-        return mm(ph[0:4 * peers].astype(BF16), w[...])
+        return mm_nt(ph[0:4 * peers].astype(BF16), w[...])
 
     def to_partner(index, src, dst):
         return remote(src, dst, bs.at[index], br.at[index], {"tp": u})
+
+    def to_other(i, half, slot):
+        ref = c_i.at[half, slot]
+        return remote(ref, ref, xs.at[i], xr.at[i], {"col": lax.rem(c + i, NCOL), "tp": u})
+
+    def send_pooled_img():
+        @pl.loop(0, NCOL)
+        def _(i):
+            to_other(i, t, c).start()
+
+        send_img(CC, lambda to: c_i.at[t, c], c_i.at[t])
+
+    def recv_pooled_img():
+        @pl.loop(0, NCOL)
+        def _(i):
+            to_other(i, u, lax.rem(c + NCOL - i, NCOL)).wait_recv()
+
+        recv_img(CC, c_i.at[t])
 
     def norm_of(pool):
         inv = lax.rsqrt(jnp.sum(pool * pool, axis=-1, keepdims=True) + 1e-6)
@@ -337,15 +434,9 @@
 
     def loss():
         for p in range(NCOL):
-            pxall_i[4 * p:4 * p + 4, :] = px_i[p]
+            pool_i[:, 256 * p:256 * (p + 1)] = c_i[0, p].astype(F32) + c_i[1, p].astype(F32)
         for p in range(NROW):
-            pxall_t[4 * p:4 * p + 4, :] = px_t[p]
-        for p in range(NCOL):
-            at = slice(256 * p, 256 * (p + 1))
-            pool_i[:, at] = pxall_i[:, at] + c_i[p].astype(F32)
-        for p in range(NROW):
-            at = slice(128 * p, 128 * (p + 1))
-            pool_t[:, at] = pxall_t[:, at] + c_t[p].astype(F32)
+            pool_t[:, 128 * p:128 * (p + 1)] = c_t[p].astype(F32)
         emb_i, inv_i = norm_of(pool_i[...])
         emb_t, inv_t = norm_of(pool_t[...])
         ih, il = split(emb_i)
@@ -379,7 +470,7 @@
         g_t = two[0:nt] + two[nt:] + mm(dh, il)
         q_i = jnp.sum(dl * cos, axis=-1, keepdims=True)
         q_t = jnp.sum(dl_t * cos_t, axis=-1, keepdims=True)
-        part_i = (g_i - emb_i * q_i) * (temp * inv_i / pxall_i[:, PAD:PAD + 1])
+        part_i = (g_i - emb_i * q_i) * (temp * inv_i / pxall_i[:, 256:257])
         part_t = (g_t - emb_t * q_t) * (temp * inv_t * (1.0 / TOKENS))
         for p in range(NCOL):
             es_i[p] = part_i[:, 256 * p:256 * (p + 1)].astype(BF16)
@@ -395,7 +486,7 @@
         for p in range(1, peers):
             total = total + src[p].astype(F32)
         hi, lo = split(total)
-        hidden = mm_nt(hi, w[...])
+        hidden = mm(hi, w[...])
         hi, lo = hi.astype(F32), lo.astype(F32)
         for p in range(peers):
             rows = slice(4 * p, 4 * p + 4)
@@ -423,27 +514,44 @@
         for q in range(4):
             dst[4 * u + q, 0:IPD, :] = stage[4 * q:4 * q + 4, :]
 
-    def back_img(half):
-        @pl.loop(0, 4)
-        def _(n):
+    def back(piece, add, bufs):
+        piece(0, bufs[0])
+        piece(1, bufs[1])
+        total = add(0, bufs[0])
+        piece(2, bufs[0])
+        total += add(1, bufs[1])
+        piece(3, bufs[1])
+        total += add(2, bufs[0])
+        return total + add(3, bufs[1])
+
+    def back_img(own, half):
+        def piece(n, dst):
             for h in range(2):
                 for i in range(IPD):
                     at = slice(SLOTS * i, SLOTS * (i + 1))
                     slope = sp_i[half, 2 * n + h, at, :]
-                    dpre_i[at, 256 * h:256 * (h + 1)] = (
+                    dst[at, 256 * h:256 * (h + 1)] = (
                         slope * dh_i[4 * half + n, i:i + 1, 256 * h:256 * (h + 1)]
                     ).astype(BF16)
-            w = jnp.concatenate([wi[half, 4 * n + j, pl.ds(2 * t, 2)].reshape(HALF, 128) for j in range(4)], axis=1)
-            acc_i[...] += mm_nt(dpre_i[...], w)
+
+        def add(n, src):
+            ds = [lax.rem(2 * t + j + SIDE - zlo, SIDE) for j in (0, 1)]
+            w = jnp.concatenate([img_rows(own, half, 4 * n + j, ds) for j in range(4)], axis=1)
+            return mm_nt(src[...], w)
+
+        return back(piece, add, (dpre_i, dpre_i2))
 
     def back_txt(half):
-        @pl.loop(0, 4)
-        def _(n):
+        def piece(n, dst):
             for i in range(IPD):
                 at = slice(TOKENS * i, TOKENS * (i + 1))
-                dpre_t[at, :] = (sp_t[half, n, at, :] * dh_t[4 * half + n, i:i + 1, :]).astype(BF16)
-            w = wt[half, pl.ds(8 * t, 8), :, :, pl.ds(pl.multiple_of(512 * n, 512), 512)].reshape(HALF, 512)
-            acc_t[...] += mm_nt(dpre_t[...], w)
+                dst[at, :] = (sp_t[half, n, at, :] * dh_t[4 * half + n, i:i + 1, :]).astype(BF16)
+
+        def add(n, src):
+            w = wt[half, pl.ds(8 * t, 8), :, :, pl.ds(512 * n, 512)].reshape(HALF, 512)
+            return mm_nt(src[...], w)
+
+        return back(piece, add, (dpre_t, dpre_t2))
 
     def token_part(src, wide):
         if wide:
@@ -462,133 +570,169 @@
 
     def finish_txt():
         token = token_part(f_t, False)
+        acc_t[...] += back_txt(u)
         for i in range(IPD):
             at = slice(TOKENS * i, TOKENS * (i + 1))
             out_t[at, :] = (acc_t[at, :] + token[i:i + 1]).astype(BF16)
-        copy = pltpu.make_async_copy(out_t, ot_h, ls.at[6])
-        copy.start()
-        return copy
 
     def finish_img():
         token = token_part(f_i, True)
+        acc_i[...] += back_img(False, u)
         for i in range(IPD):
             at = slice(SLOTS * i, SLOTS * (i + 1))
             out_i[at, :] = (acc_i[at, :] + jnp.where(live(i, HALF), token[i:i + 1], 0.0)).astype(BF16)
-        copy = pltpu.make_async_copy(out_i, oi_h, ls.at[7])
-        copy.start()
-        return copy
 
     def await_z_same():
         @pl.loop(1, SIDE)
         def _(i):
-            z_img_same(i, turn(zlo, SIDE - i)).wait_recv()
+            z_img_same(i, i).wait_recv()
+
+    def await_z_whole():
+        locals_[1].wait()
+        whole_to_sibling(0, k).start()
+
+        @pl.loop(1, SIDE)
+        def _(i):
+            z_img_whole(i, SIDE - i).wait_recv()
+            whole_to_sibling(SIDE - i, k).start()
+
+    def await_sibling_whole():
+        own_to_sibling(1 - k).wait_recv()
+
+        @pl.loop(0, SIDE)
+        def _(i):
+            whole_to_sibling(i, 1 - k).wait_recv()
 
     def await_z_other():
         @pl.loop(0, SIDE)
         def _(i):
-            z_img_other(i, u, turn(zlo, SIDE - i)).wait_recv()
+            z_img_other(i, u, i).wait_recv()
 
     locals_[0].wait()
     t0.s1()
-    z_later()
+    z_txt_each(lambda copy: copy.start())
+
+    @pl.loop(1, SIDE)
+    def _(i):
+        z_img_whole(i, SIDE - i).start()
+
+    t0.s2()
+    t0.s2b()
+    await_z_same()
+    i0.s1()
+
+    @pl.loop(0, NROW)
+    def _(i):
+        own_block(i).wait()
+
+    own_to_sibling(k).start()
     tail[...] = jnp.zeros_like(tail)
     dtp[...] = jnp.zeros_like(dtp)
+    t0.s3(0)
+    i0.s2()
     local_part()
-    t0.s2()
-    t0.s2b()
-    locals_[1].wait()
-    await_z_same()
-    i0.s1()
+    z_later()
+    t0.s3(3, 1)
+    i0.s2b()
+    t0.s3(2)
     pad_out()
-    t0.s3()
-    i0.s2()
     t0.s4()
-    i0.s2b()
+    i0.s3(0, 3)
     t0.from_sibling()
     fwd_txt(t, True)
     send_hidden_txt()
-    i0.s3()
-    z_txt(u).wait_recv()
+    await_z_whole()
+    z_txt(u, zlo, 8).wait_recv()
     t1.s1()
-    i0.s4()
-    t1.s2()
-    t1.s2b()
-    await_z_other()
-    i1.s1()
-    i0.from_sibling()
-    fwd_img(t, True)
-    send_hidden_img()
+    i0.s3(1, 2)
     recv_txt(AA, a_t)
     bs_t[...] = projected(a_t, NROW, wot)
     to_partner(1, bs_t, br_t).start()
+    await_sibling_whole()
+    fwd_img(i0, True, 0, 1)
+    i0.s4()
+    fwd_img(i0, True, 1, 2)
+    t1.s2()
+    to_partner(1, bs_t, br_t).wait_recv()
+    recv_txt(PX, px_t)
+    c_t[r] = (bs_t[...] + br_t[...] + pooled_tokens(px_t, NROW, 128, pxall_t)).astype(BF16)
+    send_txt(CC, lambda to: c_t.at[r], c_t)
+    fwd_img(i0, True, 2, 4)
+    send_hidden_img()
+    t1.s2b()
+    t1.s3(0)
     recv_img(AA, a_i)
-    bs_i[...] = projected(a_i, NCOL, woi)
-    to_partner(0, bs_i, br_i).start()
+    recv_img(PX, px_i)
+    tokens = jnp.where(t == 0, pooled_tokens(px_i, NCOL, 256, pxall_i), 0.0)
+    c_i[t, c] = (projected(a_i, NCOL, woi) + tokens).astype(BF16)
+    send_pooled_img()
+    t1.s3(3, 1)
+    recv_txt(CC, c_t)
+    t1.s3(2)
+    await_z_other()
+    i1.s1()
+    t1.s4()
+    recv_pooled_img()
+    loss()
     i1.s2()
-    to_partner(1, bs_t, br_t).wait_recv()
-    c_t[r] = (bs_t[...] + br_t[...]).astype(BF16)
-    send_txt(CC, lambda to: c_t.at[r], c_t)
-    to_partner(0, bs_i, br_i).wait_recv()
-    c_i[c] = (bs_i[...] + br_i[...]).astype(BF16)
-    send_img(CC, lambda to: c_i.at[c], c_i)
-    t1.s3()
     i1.s2b()
-    recv_img(PX, px_i)
-    recv_txt(PX, px_t)
-    recv_img(CC, c_i)
-    recv_txt(CC, c_t)
-    loss()
-    t1.s4()
+    t1.from_sibling()
+    fwd_txt(u, False)
+    i1.s3(0)
     recv_img(EE, e_i)
     dhidden(e_i, NCOL, woi, fs_i, True)
     f_i[c] = fs_i[c]
     send_img(FF, lambda to: fs_i.at[to], f_i)
+    i1.s3(3)
     recv_txt(EE, e_t)
     dhidden(e_t, NROW, wot, fs_t, False)
     f_t[r] = fs_t[r]
     send_txt(FF, lambda to: fs_t.at[to], f_t)
-    i1.s3()
+    i1.s3(1, 2)
+    fwd_img(i1, False, 0, 1)
     recv_img(FF, f_i)
-    f2s[0:16, :] = hidden_sum(f_i, NCOL, dh_i)
+    f2s[0] = hidden_sum(f_i, NCOL, dh_i)
+    to_partner(2, f2s.at[0], f2r.at[0]).start()
+    i1.s4()
+    acc_i[...] = back_img(True, t)
     recv_txt(FF, f_t)
-    f2s[16:32, :] = hidden_sum(f_t, NROW, dh_t)
-    to_partner(2, f2s, f2r).start()
-    back_txt(t)
-    i1.s4()
-    back_img(t)
-    t1.from_sibling()
-    fwd_txt(u, False)
-    to_partner(2, f2s, f2r).wait_recv()
-    hidden_other(f2r[0:16, :], dh_i)
-    hidden_other(f2r[16:32, :], dh_t)
-    back_txt(u)
-    done_t = finish_txt()
-    i1.from_sibling()
-    fwd_img(u, False)
-    back_img(u)
-    done_i = finish_img()
+    f2s[1] = hidden_sum(f_t, NROW, dh_t)
+    to_partner(3, f2s.at[1], f2r.at[1]).start()
+    acc_t[...] = back_txt(t)
+    fwd_img(i1, False, 1, 4)
+    to_partner(2, f2s.at[0], f2r.at[0]).wait_recv()
+    hidden_other(f2r[0], dh_i)
+    finish_img()
+    to_partner(3, f2s.at[1], f2r.at[1]).wait_recv()
+    hidden_other(f2r[1], dh_t)
+    finish_txt()
 
     @pl.loop(1, SIDE)
     def _(i):
-        z_img_same(i, zlo).wait_send()
+        z_img_same(i, SIDE - i).wait_send()
+        z_img_whole(i, SIDE - i).wait_send()
 
     @pl.loop(0, SIDE)
     def _(i):
-        z_img_other(i, t, zlo).wait_send()
-
-    z_txt(t).wait_send()
+        whole_to_sibling(i, k).wait_send()
+        z_img_other(i, t, lax.rem(SIDE - i, SIDE)).wait_send()
+
+    z_txt_each(lambda copy: copy.wait_send())
+    own_to_sibling(k).wait_send()
     for batch in (t0, i0, t1, i1):
         batch.drain()
-    to_partner(0, bs_i, br_i).wait_send()
+    @pl.loop(0, NCOL)
+    def _(i):
+        to_other(i, t, c).wait_send()
+
     to_partner(1, bs_t, br_t).wait_send()
-    to_partner(2, f2s, f2r).wait_send()
-    drain_small(PX, px_i, px_t)
+    to_partner(2, f2s.at[0], f2r.at[0]).wait_send()
+    to_partner(3, f2s.at[1], f2r.at[1]).wait_send()
+    drain_small(PX, pxs_i, pxs_t)
     drain_small(AA, a_i, a_t)
-    drain_small(CC, c_i, c_t)
+    drain_small(CC, c_i.at[t], c_t)
     drain_small(EE, es_i, es_t)
     drain_small(FF, fs_i, fs_t)
-    done_t.wait()
-    done_i.wait()
 
 
 def vm(*shape, dtype=F32):
@@ -596,27 +740,28 @@
 
 
 SCRATCH = [
-    vm(2, NROW, 4, 2, 192, 128, dtype=BF16), vm(2, NROW, 2, 48, HID, dtype=BF16),
+    vm(2, NROW, 4, 2, 192, 128, dtype=BF16), vm(4, 2, RHO, HID, dtype=BF16), vm(2, NROW, 2, 48, HID, dtype=BF16),
     vm(MI, D, dtype=BF16), vm(MT, D, dtype=BF16),
-    vm(HID, 192, dtype=BF16), vm(HID, 96, dtype=BF16), vm(HID, 256, dtype=BF16), vm(HID, 128, dtype=BF16),
+    vm(192, HID, dtype=BF16), vm(96, HID, dtype=BF16), vm(256, HID, dtype=BF16), vm(128, HID, dtype=BF16),
     vm(384, 512, dtype=BF16),
     vm(2, 8, MI, 256), vm(2, 4, MT, 512), vm(8, 8, 256), vm(4, 8, 512),
     vm(MI, HALF), vm(MT, HALF), vm(MI, 512, dtype=BF16), vm(MT, 512, dtype=BF16),
-    vm(MI, HALF, dtype=BF16), vm(MT, HALF, dtype=BF16),
-    vm(NCOL, IPD, PAD + 128), vm(NROW, IPD, PAD), vm(32, PAD + 128), vm(64, PAD),
+    vm(MI, 512, dtype=BF16), vm(MT, 512, dtype=BF16),
+    vm(NCOL, IPD, 384), vm(NROW, IPD, 128), vm(NCOL, IPD, 384), vm(NROW, IPD, 128), vm(32, 384), vm(64, 128),
     vm(NCOL, 16, 512, dtype=BF16), vm(NROW, 16, 512, dtype=BF16), vm(16, 512), vm(64, HID),
-    vm(32, 256), vm(64, 128), vm(32, 256), vm(64, 128),
-    vm(NCOL, 32, 256, dtype=BF16), vm(NROW, 64, 128, dtype=BF16), vm(32, PAD), vm(64, PAD),
+    vm(64, 128), vm(64, 128),
+    vm(2, NCOL, 32, 256, dtype=BF16), vm(NROW, 64, 128, dtype=BF16), vm(32, PAD), vm(64, PAD),
     vm(NCOL, 32, 256, dtype=BF16), vm(NROW, 64, 128, dtype=BF16),
     vm(NCOL, 32, 256, dtype=BF16), vm(NROW, 64, 128, dtype=BF16),
     vm(NCOL, 16, 640, dtype=BF16), vm(NROW, 16, 640, dtype=BF16),
     vm(NCOL, 16, 640, dtype=BF16), vm(NROW, 16, 640, dtype=BF16),
-    vm(16, 128), vm(32, 512, dtype=BF16), vm(32, 512, dtype=BF16), vm(8, 8, 512), vm(8, 8, 512), vm(16, 1024),
+    vm(16, 128), vm(2, 16, 512, dtype=BF16), vm(2, 16, 512, dtype=BF16), vm(8, 8, 512), vm(8, 8, 512), vm(16, 1024),
     pltpu.SemaphoreType.DMA((4, 32)), pltpu.SemaphoreType.DMA((4, 32)),
-    pltpu.SemaphoreType.DMA((9,)), pltpu.SemaphoreType.DMA((9,)),
-    pltpu.SemaphoreType.DMA((8,)),
+    pltpu.SemaphoreType.DMA((17,)), pltpu.SemaphoreType.DMA((17,)),
+    pltpu.SemaphoreType.DMA((12,)), pltpu.SemaphoreType.DMA((NROW,)),
     pltpu.SemaphoreType.DMA((5, 24)), pltpu.SemaphoreType.DMA((5, 24)),
-    pltpu.SemaphoreType.DMA((3,)), pltpu.SemaphoreType.DMA((3,)),
+    pltpu.SemaphoreType.DMA((4,)), pltpu.SemaphoreType.DMA((4,)),
+    pltpu.SemaphoreType.DMA((NCOL,)), pltpu.SemaphoreType.DMA((NCOL,)),
 ]
 
 
@@ -625,17 +770,17 @@
     hbm = pl.BlockSpec(memory_space=pl.ANY)
     grad_i, grad_t = pl.pallas_call(
         kernel,
-        out_shape=(jax.ShapeDtypeStruct((MI, HALF), BF16), jax.ShapeDtypeStruct((MT, HALF), BF16)),
+        out_shape=(pltpu.VMEM((MI, HALF), BF16), pltpu.VMEM((MT, HALF), BF16)),
         in_specs=[smem] * 4 + [hbm] * 6,
-        out_specs=(hbm, hbm),
+        out_specs=(pl.BlockSpec(memory_space=pltpu.VMEM),) * 2,
         scratch_shapes=SCRATCH,
         compiler_params=pltpu.CompilerParams(
-            collective_id=0, has_side_effects=True, vmem_limit_bytes=60 * 2**20
+            collective_id=0, has_side_effects=True, vmem_limit_bytes=58 * 2**20
         ),
         name="towers",
     )(
         counts, partner, scale, shift, patches.reshape(MI, D), text.reshape(MT, D),
-        img_w_in, img_w_out, txt_w_in, txt_w_out,
+        img_w_in, img_w_out.T, txt_w_in, txt_w_out.T,
     )
     return grad_i.reshape(IPD, SLOTS, HALF), grad_t.reshape(IPD, TOKENS, HALF)
 

time: 134 us -> 121 us (0.903)
  Pallas kernels: 125 us -> 118 us
  local copies, waits for them, and re-layouts: 7.07 us -> 1.63 us
    pallas_call x1, Pallas kernels: 125 us -> 118 us  [shards(): pl.pallas_call(kernel, out_shape=(pltpu.VMEM((MI, HALF), BF16), pltpu.VME...]
    unnamed x6 -> x2, local copies, waits for them, and re-layouts: 7.07 us -> 1.63 us
where the time goes in v2:
time: 121 us
  Pallas kernels  118 us (98%)
  between operations  1.93 us (2%)
  local copies, waits for them, and re-layouts  1.63 us (1%)
    pallas_call x1, Pallas kernels, shards(): pl.pallas_call(kernel, out_shape=(pltpu.VMEM((MI, HALF), BF16), pltpu.VME...  118 us

profile of v2, /device:TPU:1, one launch (start us, length us, event | category | flops | bytes accessed | tf_op | source)
XLA Modules:
  0.0 121.3 jit_solution(6466581769324835895)
XLA Ops:
  1.9 117.7 %towers.1 = (bf16[512,768]{1,0:T(8,128)(2,1)S(1)}, bf16[256,768]{1,0:T(8,128)(2,1)S(1)}) custom-call(s32[4]{0:T(128)} %counts.1, s32[512]{0:T(512)} %partner.1, f32[1]{0:T(128)S(6)} %copy.16.scale, f32[1]{0:T(128)S(6)} %copy.17.shift, bf16[512,1536]{1,0:T(8,128)(2,1)} %bitcast.8, bf16[256,1536]{1,0:T(8,128)(2,1)} %bitcast.9, bf16[192,2048]{1,0:T(8,128)(2,1)} %wii_h.1, ...), custom_call_target="tpu_custom_call" | custom-call | tf_op jit(solution)/shard_map/towers/pallas_call | solution.py:771
  119.7 0.9 copy.14
  120.5 0.7 copy.15

commit v3 on v2

--- a/solution.py
+++ b/solution.py
@@ -12,7 +12,7 @@
 IPD, SLOTS, TOKENS = 4, 128, 64
 MI, MT = IPD * SLOTS, IPD * TOKENS
 PX, AA, CC, EE, FF = range(5)
-RHO = 32
+RHO = 64
 NT = (((1,), (1,)), ((), ()))
 
 
@@ -478,8 +478,8 @@
             es_t[p] = part_t[:, 128 * p:128 * (p + 1)].astype(BF16)
         e_i[c] = es_i[c]
         e_t[r] = es_t[r]
+        send_txt(EE, lambda to: es_t.at[to], e_t)
         send_img(EE, lambda to: es_i.at[to], e_i)
-        send_txt(EE, lambda to: es_t.at[to], e_t)
 
     def dhidden(src, peers, w, dst, wide):
         total = src[0].astype(F32)
@@ -607,6 +607,27 @@
         @pl.loop(0, SIDE)
         def _(i):
             z_img_other(i, u, i).wait_recv()
+
+    def drain_z():
+        @pl.loop(1, SIDE)
+        def _(i):
+            z_img_same(i, SIDE - i).wait_send()
+            z_img_whole(i, SIDE - i).wait_send()
+
+        @pl.loop(0, SIDE)
+        def _(i):
+            whole_to_sibling(i, k).wait_send()
+            z_img_other(i, t, lax.rem(SIDE - i, SIDE)).wait_send()
+
+        z_txt_each(lambda copy: copy.wait_send())
+        own_to_sibling(k).wait_send()
+
+    def drain_pooled():
+        @pl.loop(0, NCOL)
+        def _(i):
+            to_other(i, t, c).wait_send()
+
+        drain_small(CC, c_i.at[t], c_t)
 
     locals_[0].wait()
     t0.s1()
@@ -661,24 +682,31 @@
     send_hidden_img()
     t1.s2b()
     t1.s3(0)
+    t0.drain()
+    i0.drain()
     recv_img(AA, a_i)
     recv_img(PX, px_i)
     tokens = jnp.where(t == 0, pooled_tokens(px_i, NCOL, 256, pxall_i), 0.0)
     c_i[t, c] = (projected(a_i, NCOL, woi) + tokens).astype(BF16)
     send_pooled_img()
+    await_z_other()
+    i1.s1()
     t1.s3(3, 1)
     recv_txt(CC, c_t)
     t1.s3(2)
-    await_z_other()
-    i1.s1()
+    i1.s2()
     t1.s4()
+    i1.s2b()
+    drain_z()
+    drain_small(PX, pxs_i, pxs_t)
+    drain_small(AA, a_i, a_t)
+    to_partner(1, bs_t, br_t).wait_send()
     recv_pooled_img()
     loss()
-    i1.s2()
-    i1.s2b()
     t1.from_sibling()
     fwd_txt(u, False)
     i1.s3(0)
+    drain_pooled()
     recv_img(EE, e_i)
     dhidden(e_i, NCOL, woi, fs_i, True)
     f_i[c] = fs_i[c]
@@ -688,6 +716,7 @@
     dhidden(e_t, NROW, wot, fs_t, False)
     f_t[r] = fs_t[r]
     send_txt(FF, lambda to: fs_t.at[to], f_t)
+    t1.drain()
     i1.s3(1, 2)
     fwd_img(i1, False, 0, 1)
     recv_img(FF, f_i)
@@ -700,6 +729,9 @@
     to_partner(3, f2s.at[1], f2r.at[1]).start()
     acc_t[...] = back_txt(t)
     fwd_img(i1, False, 1, 4)
+    drain_small(EE, es_i, es_t)
+    drain_small(FF, fs_i, fs_t)
+    i1.drain()
     to_partner(2, f2s.at[0], f2r.at[0]).wait_recv()
     hidden_other(f2r[0], dh_i)
     finish_img()
@@ -707,32 +739,8 @@
     hidden_other(f2r[1], dh_t)
     finish_txt()
 
-    @pl.loop(1, SIDE)
-    def _(i):
-        z_img_same(i, SIDE - i).wait_send()
-        z_img_whole(i, SIDE - i).wait_send()
-
-    @pl.loop(0, SIDE)
-    def _(i):
-        whole_to_sibling(i, k).wait_send()
-        z_img_other(i, t, lax.rem(SIDE - i, SIDE)).wait_send()
-
-    z_txt_each(lambda copy: copy.wait_send())
-    own_to_sibling(k).wait_send()
-    for batch in (t0, i0, t1, i1):
-        batch.drain()
-    @pl.loop(0, NCOL)
-    def _(i):
-        to_other(i, t, c).wait_send()
-
-    to_partner(1, bs_t, br_t).wait_send()
     to_partner(2, f2s.at[0], f2r.at[0]).wait_send()
     to_partner(3, f2s.at[1], f2r.at[1]).wait_send()
-    drain_small(PX, pxs_i, pxs_t)
-    drain_small(AA, a_i, a_t)
-    drain_small(CC, c_i.at[t], c_t)
-    drain_small(EE, es_i, es_t)
-    drain_small(FF, fs_i, fs_t)
 
 
 def vm(*shape, dtype=F32):

time: 121 us -> 118 us (0.975)
  Pallas kernels: 118 us -> 114 us
    pallas_call x1, Pallas kernels: 118 us -> 114 us  [shards(): pl.pallas_call(kernel, out_shape=(pltpu.VMEM((MI, HALF), BF16), pltpu.VME...]
where the time goes in v3:
time: 118 us
  Pallas kernels  114 us (97%)
  between operations  1.93 us (2%)
  local copies, waits for them, and re-layouts  1.63 us (1%)
    pallas_call x1, Pallas kernels, shards(): pl.pallas_call(kernel, out_shape=(pltpu.VMEM((MI, HALF), BF16), pltpu.VME...  114 us

profile of v3, /device:TPU:1, one launch (start us, length us, event | category | flops | bytes accessed | tf_op | source)
XLA Modules:
  0.0 117.9 jit_solution(1152311695485782394)
XLA Ops:
  1.9 114.3 %towers.1 = (bf16[512,768]{1,0:T(8,128)(2,1)S(1)}, bf16[256,768]{1,0:T(8,128)(2,1)S(1)}) custom-call(s32[4]{0:T(128)} %counts.1, s32[512]{0:T(512)} %partner.1, f32[1]{0:T(128)S(6)} %copy.16.scale, f32[1]{0:T(128)S(6)} %copy.17.shift, bf16[512,1536]{1,0:T(8,128)(2,1)} %bitcast.8, bf16[256,1536]{1,0:T(8,128)(2,1)} %bitcast.9, bf16[192,2048]{1,0:T(8,128)(2,1)} %wii_h.1, ...), custom_call_target="tpu_custom_call" | custom-call | tf_op jit(solution)/shard_map/towers/pallas_call | solution.py:779
  116.2 0.9 copy.14
  117.1 0.7 copy.15

commit v4 on v3

--- a/solution.py
+++ b/solution.py
@@ -12,7 +12,7 @@
 IPD, SLOTS, TOKENS = 4, 128, 64
 MI, MT = IPD * SLOTS, IPD * TOKENS
 PX, AA, CC, EE, FF = range(5)
-RHO = 64
+RHO = 96
 NT = (((1,), (1,)), ((), ()))
 
 

time: 118 us -> 124 us (1.051)
  Pallas kernels: 114 us -> 121 us
    pallas_call x1, Pallas kernels: 114 us -> 121 us  [shards(): pl.pallas_call(kernel, out_shape=(pltpu.VMEM((MI, HALF), BF16), pltpu.VME...]
where the time goes in v4:
time: 124 us
  Pallas kernels  121 us (98%)
  between operations  1.93 us (2%)
  local copies, waits for them, and re-layouts  1.63 us (1%)
    pallas_call x1, Pallas kernels, shards(): pl.pallas_call(kernel, out_shape=(pltpu.VMEM((MI, HALF), BF16), pltpu.VME...  121 us

profile of v4, /device:TPU:1, one launch (start us, length us, event | category | flops | bytes accessed | tf_op | source)
XLA Modules:
  0.0 124.1 jit_solution(13428948437598328161)
XLA Ops:
  1.9 120.5 %towers.1 = (bf16[512,768]{1,0:T(8,128)(2,1)S(1)}, bf16[256,768]{1,0:T(8,128)(2,1)S(1)}) custom-call(s32[4]{0:T(128)} %counts.1, s32[512]{0:T(512)} %partner.1, f32[1]{0:T(128)S(6)} %copy.16.scale, f32[1]{0:T(128)S(6)} %copy.17.shift, bf16[512,1536]{1,0:T(8,128)(2,1)} %bitcast.8, bf16[256,1536]{1,0:T(8,128)(2,1)} %bitcast.9, bf16[192,2048]{1,0:T(8,128)(2,1)} %wii_h.1, ...), custom_call_target="tpu_custom_call" | custom-call | tf_op jit(solution)/shard_map/towers/pallas_call | solution.py:779
  122.4 0.9 copy.14
  123.3 0.7 copy.15
